TPU v7x, 32 devices: a whole 2x2x4 slice. The times are simulated.
32 devices in a mesh: grp: 2 (over x), cell: 16 (over z, y, core).
Axes of the slice: x: 2, y: 2, z: 4, core: 2. Of those that a mesh axis runs over, the one named last changes fastest.
Arguments:
- fields: bfloat16 [8192, 3, 8192], P(('grp', 'cell')), parts along dimension 0, may hold values from -6 to 6
- horiz: float32 [16384], P(('grp', 'cell')), parts along dimension 0, may hold values from 0.2 to 1
- vertical: float32 [16384], P(('grp', 'cell')), parts along dimension 0, may hold values from 1.5 to 6
- tilt_angle: float32 [16384], P(('grp', 'cell')), parts along dimension 0, may hold values from 0.2 to 1.4
- azimuth: float32 [16384], P(('grp', 'cell')), parts along dimension 0, may hold values from -3.140625 to 3.140625
- electrode_quads: int32 [4096, 4], P('grp'), parts along dimension 0, may hold values from 0 to 4095, as said below
Outputs:
- jacobian: bfloat16 [4096, 4, 8192], P('grp', None, 'cell'), parts along dimension 0
- coverage: float32 [16384], P(('grp', 'cell')), parts along dimension 0
There are 2 independent parts, one for each index of `grp`. A program takes and returns all parts, laid end to end along the dimension named above; each array names one. Nothing has to cross between parts.
Inputs may be any that keep to these rules, and one draw needn't show every extreme that they name: `electrode_quads`: each row names four different electrodes.
All inputs are finite; a program needn't handle non-finite values.
Results may differ from a plain program's by a relative error of at most 0.001.
Values may be sent and summed in bfloat16 or wider, within the bound.
A program may use at most 192 MiB of HBM per device.

v0:
```python
import jax
import jax.numpy as jnp
from jax import lax
from jax.sharding import PartitionSpec as P


def sensitivity(grads, horiz, vertical, tilt_angle, azimuth, rows):

    def pick(column):
        return jnp.take(grads, rows[:, column], axis=0).astype(jnp.float32)

    source = pick(0) - pick(1)
    receiver = pick(2) - pick(3)
    sin_t = jnp.sin(tilt_angle)
    cos_t = jnp.cos(tilt_angle)
    sin_p = jnp.sin(azimuth)
    cos_p = jnp.cos(azimuth)
    axis_dir = jnp.stack([sin_t * cos_p, sin_t * sin_p, cos_t])
    tilt_dir = jnp.stack([cos_t * cos_p, cos_t * sin_p, -sin_t])
    turn_dir = jnp.stack([-sin_t * sin_p, sin_t * cos_p, jnp.zeros_like(sin_t)])

    def along(field, direction):
        return jnp.sum(field * direction[None], axis=1)

    s_axis = along(source, axis_dir)
    r_axis = along(receiver, axis_dir)
    s_tilt = along(source, tilt_dir)
    r_tilt = along(receiver, tilt_dir)
    s_turn = along(source, turn_dir)
    r_turn = along(receiver, turn_dir)
    inner = jnp.sum(source * receiver, axis=1)
    contrast = vertical - horiz
    return jnp.stack(
        [
            -horiz * (inner - s_axis * r_axis),
            -vertical * s_axis * r_axis,
            -contrast * (s_tilt * r_axis + s_axis * r_tilt),
            -contrast * (s_turn * r_axis + s_axis * r_turn),
        ],
        axis=1,
    )


def local(fields, horiz, vertical, tilt_angle, azimuth, electrode_quads):
    shards = lax.axis_size("cell")
    cell_dev = horiz.shape[0]
    local_fields = lax.all_to_all(fields, "cell", split_axis=2, concat_axis=0, tiled=True)
    values = sensitivity(local_fields, horiz, vertical, tilt_angle, azimuth, electrode_quads)
    partial_sq = jnp.sum(values * values, axis=(1, 2))
    total_sq = lax.psum(partial_sq, "cell")
    meansq = total_sq / (4.0 * cell_dev * shards)
    normed = values * lax.rsqrt(meansq + 1e-06)[:, None, None]
    return (normed.astype(jnp.bfloat16), jnp.sum(normed * normed, axis=(0, 1)))


def solution(mesh):
    placed = (
        P(("grp", "cell"), None, None),
        P(("grp", "cell")),
        P(("grp", "cell")),
        P(("grp", "cell")),
        P(("grp", "cell")),
        P("grp", None),
    )
    return jax.shard_map(
        local,
        mesh=mesh,
        in_specs=placed,
        out_specs=(P("grp", None, "cell"), P(("grp", "cell"))),
        check_vma=False,
    )
```

profile of v0, /device:TPU:0, one launch (start us, length us, event | category | flops | bytes accessed | tf_op | source)
XLA Modules:
  0.0 745.1 jit_solution(583494292606352755)
XLA Ops:
  0.6 25.0 %copy.16 = bf16[256,3,8192]{0,1,2:T(4,128)(2,1)} copy(bf16[256,3,8192]{2,0,1:T(8,128)(2,1)} %param.8) | data formatting | bytes 25165824 | tf_op args[0]
  25.6 0.0 copy-start.5
  25.6 0.0 copy-start.6
  25.6 0.0 copy-start.3
  25.6 0.0 copy-start.4
  25.6 0.0 copy-start.2
  25.6 7.6 %all-to-all-start = ((bf16[256,3,8192]{0,1,2:T(4,128)(2,1)}), bf16[256,3,8192]{0,1,2:T(4,128)(2,1)}, u32[]{:S(2)}, u32[]{:S(2)}) async-start(bf16[256,3,8192]{0,1,2:T(4,128)(2,1)} %copy.16), calls=%async_computation | async-start | bytes 33554432 | tf_op jit(solution)/shard_map/all_to_all | solution.py:47
  33.2 0.1 pad.6.clone
  33.3 0.0 copy-done.5
  33.3 0.0 copy-done.6
  33.4 0.0 copy-done.3
  33.4 0.0 copy-done.4
  33.4 0.0 copy-done.2
  33.5 0.1 pad_maximum_fusion.1
  33.6 296.4 %all-to-all-done = bf16[256,3,8192]{0,1,2:T(4,128)(2,1)} async-done(((bf16[256,3,8192]{0,1,2:T(4,128)(2,1)}), bf16[256,3,8192]{0,1,2:T(4,128)(2,1)}, u32[]{:S(2)}, u32[]{:S(2)}) %all-to-all-start) | async-done | bytes 12582944 | tf_op jit(solution)/shard_map/all_to_all | solution.py:47
  330.0 13.2 %copy.17 = bf16[256,3,8192]{0,2,1:T(8,128)(2,1)} copy(bf16[256,3,8192]{0,1,2:T(4,128)(2,1)} %all-to-all-done) | data formatting | bytes 25165824 | tf_op jit(solution)/shard_map/all_to_all | solution.py:47
  343.1 16.6 %copy.18 = bf16[16,256,3,512]{3,1,0,2:T(8,128)(2,1)} copy(bf16[16,256,3,512]{1,3,0,2:T(8,128)(2,1)} %bitcast.54) | data formatting | bytes 25165824 | tf_op jit(solution)/shard_map/all_to_all | solution.py:47
  359.7 18.9 %copy.19 = bf16[4096,3,512]{2,1,0:T(4,128)(2,1)} copy(bf16[4096,3,512]{2,0,1:T(8,128)(2,1)} %bitcast.55) | data formatting | bytes 25165824 | tf_op jit(solution)/shard_map/all_to_all | solution.py:47
  378.6 26.7 %gather_fusion = bf16[2048,3,512]{2,1,0:T(4,128)(2,1)} fusion(bf16[4096,3,512]{2,1,0:T(4,128)(2,1)} %copy.19, s32[2048]{0:T(1024)S(1)} %fusion.6), kind=kCustom, calls=%fused_computation.clone | custom fusion | bytes 12591104 | tf_op jit(solution)/shard_map/jit(_take)/gather | solution.py:10
  405.2 26.9 %gather_fusion.1 = bf16[2048,3,512]{2,1,0:T(4,128)(2,1)} fusion(bf16[4096,3,512]{2,1,0:T(4,128)(2,1)} %copy.19, s32[2048]{0:T(1024)S(1)} %fusion.7), kind=kCustom, calls=%fused_computation.1.clone | custom fusion | bytes 12591104 | tf_op jit(solution)/shard_map/jit(_take)/gather | solution.py:10
  432.1 27.0 %gather_fusion.2 = bf16[2048,3,512]{2,1,0:T(4,128)(2,1)} fusion(bf16[4096,3,512]{2,1,0:T(4,128)(2,1)} %copy.19, s32[2048]{0:T(1024)S(1)} %fusion.8), kind=kCustom, calls=%fused_computation.2.clone | custom fusion | bytes 12591104 | tf_op jit(solution)/shard_map/jit(_take)/gather | solution.py:10
  459.1 26.8 %gather_fusion.3 = bf16[2048,3,512]{2,1,0:T(4,128)(2,1)} fusion(bf16[4096,3,512]{2,1,0:T(4,128)(2,1)} %copy.19, s32[2048]{0:T(1024)S(1)} %fusion.9), kind=kCustom, calls=%fused_computation.3.clone | custom fusion | bytes 12591104 | tf_op jit(solution)/shard_map/jit(_take)/gather | solution.py:10
  485.9 103.7 %multiply_reduce_fusion.8 = (f32[2048,512]{1,0:T(8,128)}, f32[2048,512]{1,0:T(8,128)}, f32[2048,512]{1,0:T(8,128)}, f32[2048,512]{1,0:T(8,128)}, f32[2048,512]{1...) fusion(bf16[2048,3,512]{2,1,0:T(4,128)(2,1)} %gather_fusion, pred[2048]{0:T(1024)(128)(4,1)S(1)} %get-tuple-element.48, ...), kind=kLoop, calls=%fused_computation.13 | loop fusion | flops 68157440 | bytes 54552576 | tf_op jit(solution)/shard_map/reduce_sum | solution.py:31
  589.6 14.0 %fusion.5 = (f32[2048,1,512]{2,0,1:T(8,128)S(1)}, f32[2048,1,512]{2,0,1:T(8,128)S(1)}, f32[2048,1,512]{2,0,1:T(8,128)}, f32[2048,1,512]{2,0,1:T(8,128)}) fusion(f32[2048,512]{1,0:T(8,128)} %get-tuple-element.14, f32[2048,512]{1,0:T(8,128)} %get-tuple-element.15, f32[2048,512]{1,0:T(8,128)} %get-tuple-element.9, f32[512]{0:T(512)S(1)} %get-tuple-element.34, ...), kind=kLoop, calls=%fused_computation.32 | loop fusion | flops 13631488 | bytes 46143488 | tf_op jit(solution)/shard_map/mul | solution.py:35
  603.6 0.0 copy-start
  603.6 0.0 copy-start.1
  603.6 2.0 copy-done
  605.5 1.2 copy-done.1
  606.8 4.6 multiply_reduce_fusion.1
  611.4 98.9 %psum.7 = f32[2048]{0:T(1024)S(1)} all-reduce(f32[2048]{0:T(1024)S(1)} %multiply_reduce_fusion.1), channel_id=1, replica_groups=mesh['grp'=2,'cell'=16] {'cell'}, use_global_device_ids=true, to_apply=%region_8.10 | all-reduce | flops 2048 | bytes 16384 | tf_op jit(solution)/shard_map/psum | solution.py:50
  710.3 7.5 %multiply_reduce_fusion = (f32[512]{0:T(512)}, bf16[2048,4,512]{2,0,1:T(8,128)(2,1)S(1)}) fusion(f32[2048]{0:T(1024)S(1)} %add_rsqrt_fusion, f32[2048,1,512]{2,0,1:T(8,128)} %get-tuple-element.22, f32[2048,1,512]{2,0,1:T(8,128)} %get-tuple-element.23, f32[2048,1,512]{2,0,1:T(8,128)} %copy-done.1, f32[2048,1,512]{2,0,1:T(8,128)} %copy-done), kind=kLoop, calls=%fused_computation.5 | loop fusion | flops 29359616 | bytes 25176064 | tf_op jit(solution)/shard_map/reduce_sum | solution.py:53
  717.8 27.3 %copy.23 = bf16[2048,4,512]{2,1,0:T(4,128)(2,1)} copy(bf16[2048,4,512]{2,0,1:T(8,128)(2,1)S(1)} %get-tuple-element.17) | data formatting | bytes 16777216
  (12 shorter events, 0.2 us)
Async XLA Ops:
  25.6 7.7 %copy-start.5 = (f32[512]{0:T(512)S(1)}, f32[512]{0:T(512)}, u32[]{:S(2)}) copy-start(f32[512]{0:T(512)} %param.11) | copy-start | bytes 6148
  25.6 7.7 %copy-start.6 = (f32[512]{0:T(512)S(1)}, f32[512]{0:T(512)}, u32[]{:S(2)}) copy-start(f32[512]{0:T(512)} %param.12) | copy-start | bytes 6148
  25.6 7.8 %copy-start.3 = (f32[512]{0:T(512)S(1)}, f32[512]{0:T(512)}, u32[]{:S(2)}) copy-start(f32[512]{0:T(512)} %param.9) | copy-start | bytes 6148
  25.6 7.8 %copy-start.4 = (f32[512]{0:T(512)S(1)}, f32[512]{0:T(512)}, u32[]{:S(2)}) copy-start(f32[512]{0:T(512)} %param.10) | copy-start | bytes 6148
  25.6 7.8 %copy-start.2 = (s32[2048,4]{0,1:T(4,128)S(1)}, s32[2048,4]{0,1:T(4,128)}, u32[]{:S(2)}) copy-start(s32[2048,4]{0,1:T(4,128)} %param.13) | copy-start | bytes 98308
  25.6 304.4 %all-to-all-start = ((bf16[256,3,8192]{0,1,2:T(4,128)(2,1)}), bf16[256,3,8192]{0,1,2:T(4,128)(2,1)}, u32[]{:S(2)}, u32[]{:S(2)}) async-start(bf16[256,3,8192]{0,1,2:T(4,128)(2,1)} %copy.16), calls=%async_computation | async-start | bytes 33554432 | tf_op jit(solution)/shard_map/all_to_all | solution.py:47
  603.6 2.0 copy-start
  603.6 3.2 copy-start.1
where the time goes:
time: 747 us; the launch traced here: 745 us
  waiting for transfers between devices  296 us (40%)
  local copies, waits for them, and re-layouts  212 us (28%)
  other arithmetic  130 us (17%)
  blocking collectives  98.9 us (13%)
  starting transfers between devices  7.58 us (1%)
    all_to_all x1, waiting for transfers between devices, local(): lax.all_to_all(fields, 'cell', split_axis=2, concat_axis=0, tiled=True)  296 us
    gather x4, local copies, waits for them, and re-layouts, pick(): return jnp.take(grads, rows[:, column], axis=0).astype(jnp.float32)  107 us
    reduce_sum x1, other arithmetic, sensitivity(): inner = jnp.sum(source * receiver, axis=1)  104 us
    psum x1, blocking collectives, local(): total_sq = lax.psum(partial_sq, 'cell')  98.9 us
    unnamed x16, local copies, waits for them, and re-layouts  55.5 us
    all_to_all x3, local copies, waits for them, and re-layouts, local(): lax.all_to_all(fields, 'cell', split_axis=2, concat_axis=0, tiled=True)  48.6 us
  transfers between devices with their start and end apart: 1, of which 1 were waited for; matrix products, arithmetic and copies ran while one was open for 0% of the time, Pallas kernels for 0%

commit v1 on v0

--- a/solution.py
+++ b/solution.py
@@ -2,6 +2,37 @@
 import jax.numpy as jnp
 from jax import lax
 from jax.sharding import PartitionSpec as P
+
+
+def detail_packet_now(frame_in, array_dim, state):
+    lower, top = (frame_in.shape[:array_dim], frame_in.shape[array_dim + 1 :])
+    return jnp.moveaxis(frame_in.reshape(*lower, state, -1, *top), array_dim, 0)
+
+
+def _hold_modes(w_in, ndim_at):
+    w_in = jnp.moveaxis(w_in, 0, ndim_at)
+    block_next = w_in.shape
+    return w_in.reshape(
+        *block_next[:ndim_at],
+        block_next[ndim_at] * block_next[ndim_at + 1],
+        *block_next[ndim_at + 2 :]
+    )
+
+
+def do_series_here(panel, ax_name, s0, point):
+    mixed_arr = lax.axis_size(ax_name)
+    value_now = lax.axis_index(ax_name)
+    high, mat_out = (mixed_arr, value_now)
+    then = detail_packet_now(point, panel, high)
+    so_far_all = [then[mat_out]]
+    for idx in [*range(1, high)]:
+        tall = then[mat_out ^ idx]
+        so_far_all.append(
+            lax.ppermute(tall, axis_name=ax_name, perm=[(i, i ^ idx) for i in range(high)])
+        )
+    a_next = jnp.stack(so_far_all, axis=0)
+    then = a_next[mat_out ^ jnp.arange(high)]
+    return _hold_modes(then, s0)
 
 
 def sensitivity(grads, horiz, vertical, tilt_angle, azimuth, rows):
@@ -44,7 +75,7 @@
 def local(fields, horiz, vertical, tilt_angle, azimuth, electrode_quads):
     shards = lax.axis_size("cell")
     cell_dev = horiz.shape[0]
-    local_fields = lax.all_to_all(fields, "cell", split_axis=2, concat_axis=0, tiled=True)
+    local_fields = do_series_here(2, "cell", 0, fields)
     values = sensitivity(local_fields, horiz, vertical, tilt_angle, azimuth, electrode_quads)
     partial_sq = jnp.sum(values * values, axis=(1, 2))
     total_sq = lax.psum(partial_sq, "cell")

time: 747 us -> 712 us (0.953)
  waiting for transfers between devices: 296 us -> 184 us
  local copies, waits for them, and re-layouts: 212 us -> 285 us
  starting transfers between devices: 7.58 us -> 23 us
  blocking collectives: 98.9 us -> 86.6 us
    all_to_all x1 -> x0, waiting for transfers between devices: 296 us -> none  [local(): lax.all_to_all(fields, 'cell', split_axis=2, concat_axis=0, tiled=True)]
    ppermute x0 -> x15, waiting for transfers between devices: none -> 184 us  [do_series_here(): lax.ppermute(tall, axis_name=ax_name, perm=[(i, i ^ idx) for i in range(h...]
    reshape x0 -> x1, local copies, waits for them, and re-layouts: none -> 54.1 us  [_hold_modes(): w_in.reshape(*block_next[:ndim_at], block_next[ndim_at] * block_next[ndim...]
    all_to_all x3 -> x0, local copies, waits for them, and re-layouts: 48.6 us -> none  [local(): lax.all_to_all(fields, 'cell', split_axis=2, concat_axis=0, tiled=True)]
    another operation x0 -> x18, local copies, waits for them, and re-layouts: none -> 38.7 us
    ppermute x0 -> x15, starting transfers between devices: none -> 23 us  [do_series_here(): lax.ppermute(tall, axis_name=ax_name, perm=[(i, i ^ idx) for i in range(h...]
    gather x0 -> x2, local copies, waits for them, and re-layouts: none -> 17.3 us  [do_series_here(): then = a_next[mat_out ^ jnp.arange(high)]]
    unnamed x16 -> x31, local copies, waits for them, and re-layouts: 55.5 us -> 68.2 us
  transfers between devices with their start and end apart: 1 -> 15, of which waited for: 1 -> 5; matrix products, arithmetic and copies ran while one was open for 0% -> 7% of each run, Pallas kernels for 0% -> 0%
where the time goes in v1:
time: 712 us; the launch traced here: 710 us
  local copies, waits for them, and re-layouts  285 us (40%)
  waiting for transfers between devices  184 us (26%)
  other arithmetic  130 us (18%)
  blocking collectives  86.6 us (12%)
  starting transfers between devices  23 us (3%)
    ppermute x15, waiting for transfers between devices, do_series_here(): lax.ppermute(tall, axis_name=ax_name, perm=[(i, i ^ idx) for i in range(h...  184 us
    gather x4, local copies, waits for them, and re-layouts, pick(): return jnp.take(grads, rows[:, column], axis=0).astype(jnp.float32)  107 us
    reduce_sum x1, other arithmetic, sensitivity(): inner = jnp.sum(source * receiver, axis=1)  104 us
    psum x1, blocking collectives, local(): total_sq = lax.psum(partial_sq, 'cell')  86.6 us
    unnamed x31, local copies, waits for them, and re-layouts  68.2 us
    reshape x1, local copies, waits for them, and re-layouts, _hold_modes(): w_in.reshape(*block_next[:ndim_at], block_next[ndim_at] * block_next[ndim...  54.1 us
    another operation x17, local copies, waits for them, and re-layouts  37.7 us
    ppermute x15, starting transfers between devices, do_series_here(): lax.ppermute(tall, axis_name=ax_name, perm=[(i, i ^ idx) for i in range(h...  23 us
  transfers between devices with their start and end apart: 15, of which 5 were waited for; matrix products, arithmetic and copies ran while one was open for 7% of the time, Pallas kernels for 0%

profile of v1, /device:TPU:0, one launch (start us, length us, event | category | flops | bytes accessed | tf_op | source)
XLA Modules:
  0.0 710.4 jit_solution(14091153309603280939)
XLA Ops:
  0.7 16.6 %copy.10 = bf16[256,3,8192]{0,2,1:T(8,128)(2,1)} copy(bf16[256,3,8192]{2,0,1:T(8,128)(2,1)} %param.8) | data formatting | bytes 25165824 | tf_op args[0]
  17.4 8.0 %constant_dynamic-slice_fusion = (bf16[256,3,1,512]{0,3,2,1:T(8,128)(2,1)S(1)}, bf16[256,3,1,512]{0,3,2,1:T(8,128)(2,1)S(1)}, bf16[256,3,1,512]{0,3,2,1:T(8,128)...) fusion(bf16[256,3,16,512]{0,3,2,1:T(8,128)(2,1)} %bitcast.102, ...), kind=kLoop, calls=%fused_computation.68 | loop fusion | bytes 25165888 | tf_op jit(solution)/shard_map/dynamic-slice.15
  28.1 2.3 copy.13
  30.4 2.5 collective-permute-start.1
  35.4 2.3 copy.15
  42.2 2.3 copy.11
  49.1 2.3 copy.19
  51.4 2.3 copy.20
  56.0 2.3 copy.22
  62.5 2.6 collective-permute-start.5
  69.4 2.7 collective-permute-start.7
  76.2 31.6 %collective-permute-done.4 = bf16[256,3,512]{2,0,1:T(8,128)(2,1)} collective-permute-done((bf16[256,3,512]{2,0,1:T(8,128)(2,1)}, bf16[256,3,512]{2,0,1:T(8,128)(2,1)}, u32[]{:S(2)}, u32[]{:S(2)}) %collective-permute-start.4) | collective-permute-done | bytes 786464 | tf_op jit(solution)/shard_map/ppermute | solution.py:31
  107.8 4.0 collective-permute-start.9
  113.9 13.1 %collective-permute-done.5 = bf16[256,3,512]{2,0,1:T(8,128)(2,1)S(1)} collective-permute-done((bf16[256,3,512]{2,0,1:T(8,128)(2,1)}, bf16[256,3,512]{2,0,1:T(8,128)(2,1)S(1)}, u32[]{:S(2)}, u32[]{:S(2)}) %collective-permute-start.5) | collective-permute-done | bytes 786464 | tf_op jit(solution)/shard_map/ppermute | solution.py:31
  128.1 14.4 %collective-permute-done.6 = bf16[256,3,512]{2,0,1:T(8,128)(2,1)S(1)} collective-permute-done((bf16[256,3,512]{2,0,1:T(8,128)(2,1)}, bf16[256,3,512]{2,0,1:T(8,128)(2,1)S(1)}, u32[]{:S(2)}, u32[]{:S(2)}) %collective-permute-start.6) | collective-permute-done | bytes 786464 | tf_op jit(solution)/shard_map/ppermute | solution.py:31
  142.5 3.6 collective-permute-start.11
  148.4 3.5 collective-permute-start.13
  152.8 93.5 %collective-permute-done.9 = bf16[256,3,512]{2,0,1:T(8,128)(2,1)S(1)} collective-permute-done((bf16[256,3,512]{2,0,1:T(8,128)(2,1)}, bf16[256,3,512]{2,0,1:T(8,128)(2,1)S(1)}, u32[]{:S(2)}, u32[]{:S(2)}) %collective-permute-start.9) | collective-permute-done | bytes 786464 | tf_op jit(solution)/shard_map/ppermute | solution.py:31
  248.2 31.7 %collective-permute-done.10 = bf16[256,3,512]{2,0,1:T(8,128)(2,1)S(1)} collective-permute-done((bf16[256,3,512]{2,0,1:T(8,128)(2,1)}, bf16[256,3,512]{2,0,1:T(8,128)(2,1)S(1)}, u32[]{:S(2)}, u32[]{:S(2)}) %collective-permute-start.10) | collective-permute-done | bytes 786464 | tf_op jit(solution)/shard_map/ppermute | solution.py:31
  284.7 11.0 %gather_fusion = bf16[16,256,3,512]{3,1,2,0:T(8,128)(2,1)} fusion(bf16[16,256,3,512]{3,1,2,0:T(8,128)(2,1)} %bitcast_dynamic-update-slice_fusion, s32[1024]{0:T(1024)S(1)} %pad_clamp_fusion), kind=kCustom, calls=%fused_computation.4 | custom fusion | bytes 25165888 | tf_op jit(solution)/shard_map/gather | solution.py:34
  295.7 6.3 copy.27
  302.0 54.1 %copy.28 = bf16[4096,3,512]{2,1,0:T(4,128)(2,1)} copy(bf16[4096,3,512]{2,0,1:T(8,128)(2,1)S(1)} %bitcast.101) | data formatting | bytes 25165824 | tf_op jit(solution)/shard_map/reshape | solution.py:15
  356.1 26.8 %gather_fusion.2 = bf16[2048,3,512]{2,1,0:T(4,128)(2,1)} fusion(bf16[4096,3,512]{2,1,0:T(4,128)(2,1)} %copy.28, s32[2048]{0:T(1024)S(1)} %get-tuple-element.58), kind=kCustom, calls=%fused_computation.1.clone | custom fusion | bytes 12591104 | tf_op jit(solution)/shard_map/jit(_take)/gather | solution.py:41
  382.9 26.8 %gather_fusion.3 = bf16[2048,3,512]{2,1,0:T(4,128)(2,1)} fusion(bf16[4096,3,512]{2,1,0:T(4,128)(2,1)} %copy.28, s32[2048]{0:T(1024)S(1)} %get-tuple-element.59), kind=kCustom, calls=%fused_computation.2.clone | custom fusion | bytes 12591104 | tf_op jit(solution)/shard_map/jit(_take)/gather | solution.py:41
  409.7 26.8 %gather_fusion.4 = bf16[2048,3,512]{2,1,0:T(4,128)(2,1)} fusion(bf16[4096,3,512]{2,1,0:T(4,128)(2,1)} %copy.28, s32[2048]{0:T(1024)S(1)} %get-tuple-element.60), kind=kCustom, calls=%fused_computation.3.clone | custom fusion | bytes 12591104 | tf_op jit(solution)/shard_map/jit(_take)/gather | solution.py:41
  436.5 26.7 %gather_fusion.1 = bf16[2048,3,512]{2,1,0:T(4,128)(2,1)} fusion(bf16[4096,3,512]{2,1,0:T(4,128)(2,1)} %copy.28, s32[2048]{0:T(1024)S(1)} %get-tuple-element.57), kind=kCustom, calls=%fused_computation.clone | custom fusion | bytes 12591104 | tf_op jit(solution)/shard_map/jit(_take)/gather | solution.py:41
  463.2 103.7 %multiply_reduce_fusion.8 = (f32[2048,512]{1,0:T(8,128)}, f32[2048,512]{1,0:T(8,128)}, f32[2048,512]{1,0:T(8,128)}, f32[2048,512]{1,0:T(8,128)}, f32[2048,512]{1...) fusion(bf16[2048,3,512]{2,1,0:T(4,128)(2,1)} %gather_fusion.1, pred[2048]{0:T(1024)(128)(4,1)S(1)} %get-tuple-element.66, ...), kind=kLoop, calls=%fused_computation.14 | loop fusion | flops 68157440 | bytes 54552576 | tf_op jit(solution)/shard_map/reduce_sum | solution.py:62
  566.9 14.1 %fusion.5 = (f32[2048,1,512]{2,0,1:T(8,128)S(1)}, f32[2048,1,512]{2,0,1:T(8,128)S(1)}, f32[2048,1,512]{2,0,1:T(8,128)}, f32[2048,1,512]{2,0,1:T(8,128)}) fusion(f32[2048,512]{1,0:T(8,128)} %get-tuple-element.12, f32[2048,512]{1,0:T(8,128)} %get-tuple-element.13, f32[2048,512]{1,0:T(8,128)} %get-tuple-element.7, f32[512]{0:T(512)S(1)} %get-tuple-element.48, ...), kind=kLoop, calls=%fused_computation.33 | loop fusion | flops 13631488 | bytes 46143488 | tf_op jit(solution)/shard_map/mul | solution.py:66
  584.2 4.6 multiply_reduce_fusion.1
  588.8 86.6 %psum.7 = f32[2048]{0:T(1024)S(1)} all-reduce(f32[2048]{0:T(1024)S(1)} %multiply_reduce_fusion.1), channel_id=1, replica_groups=mesh['grp'=2,'cell'=16] {'cell'}, use_global_device_ids=true, to_apply=%region_8.10 | all-reduce | flops 2048 | bytes 16384 | tf_op jit(solution)/shard_map/psum | solution.py:81
  675.4 7.7 %multiply_reduce_fusion = (f32[512]{0:T(512)}, bf16[2048,4,512]{2,0,1:T(8,128)(2,1)S(1)}) fusion(f32[2048]{0:T(1024)S(1)} %add_rsqrt_fusion, f32[2048,1,512]{2,0,1:T(8,128)} %get-tuple-element.36, f32[2048,1,512]{2,0,1:T(8,128)} %get-tuple-element.37, f32[2048,1,512]{2,0,1:T(8,128)} %copy-done.1, f32[2048,1,512]{2,0,1:T(8,128)} %copy-done), kind=kLoop, calls=%fused_computation.6 | loop fusion | flops 29359616 | bytes 25176064 | tf_op jit(solution)/shard_map/reduce_sum | solution.py:84
  683.1 27.3 %copy.32 = bf16[2048,4,512]{2,1,0:T(4,128)(2,1)} copy(bf16[2048,4,512]{2,0,1:T(8,128)(2,1)S(1)} %get-tuple-element.15) | data formatting | bytes 16777216
  (73 shorter events, 45.3 us)
Async XLA Ops:
  17.3 24.5 %copy-start.2 = (s32[2048,4]{0,1:T(4,128)S(1)}, s32[2048,4]{0,1:T(4,128)}, u32[]{:S(2)}) copy-start(s32[2048,4]{0,1:T(4,128)} %param.13) | copy-start | bytes 98308
  17.3 24.6 %copy-start.5 = (f32[512]{0:T(512)S(1)}, f32[512]{0:T(512)}, u32[]{:S(2)}) copy-start(f32[512]{0:T(512)} %param.11) | copy-start | bytes 6148
  17.3 24.6 %copy-start.6 = (f32[512]{0:T(512)S(1)}, f32[512]{0:T(512)}, u32[]{:S(2)}) copy-start(f32[512]{0:T(512)} %param.12) | copy-start | bytes 6148
  17.3 24.8 %copy-start.3 = (f32[512]{0:T(512)S(1)}, f32[512]{0:T(512)}, u32[]{:S(2)}) copy-start(f32[512]{0:T(512)} %param.9) | copy-start | bytes 6148
  17.3 24.8 %copy-start.4 = (f32[512]{0:T(512)S(1)}, f32[512]{0:T(512)}, u32[]{:S(2)}) copy-start(f32[512]{0:T(512)} %param.10) | copy-start | bytes 6148
  27.7 34.8 %collective-permute-start = (bf16[256,3,512]{2,0,1:T(8,128)(2,1)}, bf16[256,3,512]{2,0,1:T(8,128)(2,1)}, u32[]{:S(2)}, u32[]{:S(2)}) collective-permute-start(bf16[256,3,512]{2,0,1:T(8,128)(2,1)} %bitcast.113), channel_id=1, source_target_pairs={{0,1},{1,0},{2,3},{3,2},{4,5},{5,4},{6,7},{7,6},{8,9},{9,8},{10,11... | collective-permute-start | bytes 2359304 | tf_op jit(solution)/shard_map/ppermute | solution.py:31
  30.4 36.7 %collective-permute-start.1 = (bf16[256,3,512]{2,0,1:T(8,128)(2,1)}, bf16[256,3,512]{2,0,1:T(8,128)(2,1)}, u32[]{:S(2)}, u32[]{:S(2)}) collective-permute-start(bf16[256,3,512]{2,0,1:T(8,128)(2,1)} %bitcast.111), channel_id=1, source_target_pairs={{0,2},{1,3},{2,0},{3,1},{4,6},{5,7},{6,4},{7,5},{8,10},{9,11},{10,... | collective-permute-start | bytes 2359304 | tf_op jit(solution)/shard_map/ppermute | solution.py:31
  35.3 34.1 %collective-permute-start.2 = (bf16[256,3,512]{2,0,1:T(8,128)(2,1)}, bf16[256,3,512]{2,0,1:T(8,128)(2,1)}, u32[]{:S(2)}, u32[]{:S(2)}) collective-permute-start(bf16[256,3,512]{2,0,1:T(8,128)(2,1)} %bitcast.110), channel_id=1, source_target_pairs={{0,3},{1,2},{2,1},{3,0},{4,7},{5,6},{6,5},{7,4},{8,11},{9,10},{10,... | collective-permute-start | bytes 2359304 | tf_op jit(solution)/shard_map/ppermute | solution.py:31
  37.7 36.4 %collective-permute-start.3 = (bf16[256,3,512]{2,0,1:T(8,128)(2,1)}, bf16[256,3,512]{2,0,1:T(8,128)(2,1)}, u32[]{:S(2)}, u32[]{:S(2)}) collective-permute-start(bf16[256,3,512]{2,0,1:T(8,128)(2,1)} %bitcast.108), channel_id=1, source_target_pairs={{0,4},{1,5},{2,6},{3,7},{4,0},{5,1},{6,2},{7,3},{8,12},{9,13},{10,... | collective-permute-start | bytes 2359304 | tf_op jit(solution)/shard_map/ppermute | solution.py:31
  41.8 66.0 %collective-permute-start.4 = (bf16[256,3,512]{2,0,1:T(8,128)(2,1)}, bf16[256,3,512]{2,0,1:T(8,128)(2,1)}, u32[]{:S(2)}, u32[]{:S(2)}) collective-permute-start(bf16[256,3,512]{2,0,1:T(8,128)(2,1)} %bitcast.106), channel_id=1, source_target_pairs={{0,5},{1,4},{2,7},{3,6},{4,1},{5,0},{6,3},{7,2},{8,13},{9,12},{10,... | collective-permute-start | bytes 2359304 | tf_op jit(solution)/shard_map/ppermute | solution.py:31
  62.5 64.5 %collective-permute-start.5 = (bf16[256,3,512]{2,0,1:T(8,128)(2,1)}, bf16[256,3,512]{2,0,1:T(8,128)(2,1)S(1)}, u32[]{:S(2)}, u32[]{:S(2)}) collective-permute-start(bf16[256,3,512]{2,0,1:T(8,128)(2,1)} %bitcast.117), channel_id=1, source_target_pairs={{0,6},{1,7},{2,4},{3,5},{4,2},{5,3},{6,0},{7,1},{8,14},{9,15},{10,... | collective-permute-start | bytes 2359304 | tf_op jit(solution)/shard_map/ppermute | solution.py:31
  67.2 75.4 %collective-permute-start.6 = (bf16[256,3,512]{2,0,1:T(8,128)(2,1)}, bf16[256,3,512]{2,0,1:T(8,128)(2,1)S(1)}, u32[]{:S(2)}, u32[]{:S(2)}) collective-permute-start(bf16[256,3,512]{2,0,1:T(8,128)(2,1)} %bitcast.116), channel_id=1, source_target_pairs={{0,7},{1,6},{2,5},{3,4},{4,3},{5,2},{6,1},{7,0},{8,15},{9,14},{10,... | collective-permute-start | bytes 2359304 | tf_op jit(solution)/shard_map/ppermute | solution.py:31
  69.4 77.7 %collective-permute-start.7 = (bf16[256,3,512]{2,0,1:T(8,128)(2,1)}, bf16[256,3,512]{2,0,1:T(8,128)(2,1)S(1)}, u32[]{:S(2)}, u32[]{:S(2)}) collective-permute-start(bf16[256,3,512]{2,0,1:T(8,128)(2,1)} %bitcast.115), channel_id=1, source_target_pairs={{0,8},{1,9},{2,10},{3,11},{4,12},{5,13},{6,14},{7,15},{8,0},{9,1},... | collective-permute-start | bytes 2359304 | tf_op jit(solution)/shard_map/ppermute | solution.py:31
  74.1 74.2 %collective-permute-start.8 = (bf16[256,3,512]{2,0,1:T(8,128)(2,1)}, bf16[256,3,512]{2,0,1:T(8,128)(2,1)S(1)}, u32[]{:S(2)}, u32[]{:S(2)}) collective-permute-start(bf16[256,3,512]{2,0,1:T(8,128)(2,1)} %bitcast.114), channel_id=1, source_target_pairs={{0,9},{1,8},{2,11},{3,10},{4,13},{5,12},{6,15},{7,14},{8,1},{9,0},... | collective-permute-start | bytes 2359304 | tf_op jit(solution)/shard_map/ppermute | solution.py:31
  107.8 138.5 %collective-permute-start.9 = (bf16[256,3,512]{2,0,1:T(8,128)(2,1)}, bf16[256,3,512]{2,0,1:T(8,128)(2,1)S(1)}, u32[]{:S(2)}, u32[]{:S(2)}) collective-permute-start(bf16[256,3,512]{2,0,1:T(8,128)(2,1)} %bitcast.112), channel_id=1, source_target_pairs={{0,10},{1,11},{2,8},{3,9},{4,14},{5,15},{6,12},{7,13},{8,2},{9,3},... | collective-permute-start | bytes 2359304 | tf_op jit(solution)/shard_map/ppermute | solution.py:31
  127.0 152.9 %collective-permute-start.10 = (bf16[256,3,512]{2,0,1:T(8,128)(2,1)}, bf16[256,3,512]{2,0,1:T(8,128)(2,1)S(1)}, u32[]{:S(2)}, u32[]{:S(2)}) collective-permute-start(bf16[256,3,512]{2,0,1:T(8,128)(2,1)} %bitcast.109), channel_id=1, source_target_pairs={{0,11},{1,10},{2,9},{3,8},{4,15},{5,14},{6,13},{7,12},{8,3},{9,2},... | collective-permute-start | bytes 2359304 | tf_op jit(solution)/shard_map/ppermute | solution.py:31
  142.5 138.4 %collective-permute-start.11 = (bf16[256,3,512]{2,0,1:T(8,128)(2,1)}, bf16[256,3,512]{2,0,1:T(8,128)(2,1)S(1)}, u32[]{:S(2)}, u32[]{:S(2)}) collective-permute-start(bf16[256,3,512]{2,0,1:T(8,128)(2,1)} %bitcast.107), channel_id=1, source_target_pairs={{0,12},{1,13},{2,14},{3,15},{4,8},{5,9},{6,10},{7,11},{8,4},{9,5},... | collective-permute-start | bytes 2359304 | tf_op jit(solution)/shard_map/ppermute | solution.py:31
  147.1 134.8 %collective-permute-start.12 = (bf16[256,3,512]{2,0,1:T(8,128)(2,1)S(1)}, bf16[256,3,512]{2,0,1:T(8,128)(2,1)S(1)}, u32[]{:S(2)}, u32[]{:S(2)}) collective-permute-start(bf16[256,3,512]{2,0,1:T(8,128)(2,1)S(1)} %bitcast.105), channel_id=1, source_target_pairs={{0,13},{1,12},{2,15},{3,14},{4,9},{5,8},{6,11},{7,10},{8,5},{9,4},... | collective-permute-start | bytes 2359304 | tf_op jit(solution)/shard_map/ppermute | solution.py:31
  148.4 134.4 %collective-permute-start.13 = (bf16[256,3,512]{2,0,1:T(8,128)(2,1)S(1)}, bf16[256,3,512]{2,0,1:T(8,128)(2,1)S(1)}, u32[]{:S(2)}, u32[]{:S(2)}) collective-permute-start(bf16[256,3,512]{2,0,1:T(8,128)(2,1)S(1)} %bitcast.104), channel_id=1, source_target_pairs={{0,14},{1,15},{2,12},{3,13},{4,10},{5,11},{6,8},{7,9},{8,6},{9,7},... | collective-permute-start | bytes 2359304 | tf_op jit(solution)/shard_map/ppermute | solution.py:31
  246.2 37.5 %collective-permute-start.14 = (bf16[256,3,512]{2,0,1:T(8,128)(2,1)S(1)}, bf16[256,3,512]{2,0,1:T(8,128)(2,1)S(1)}, u32[]{:S(2)}, u32[]{:S(2)}) collective-permute-start(bf16[256,3,512]{2,0,1:T(8,128)(2,1)S(1)} %bitcast.103), channel_id=1, source_target_pairs={{0,15},{1,14},{2,13},{3,12},{4,11},{5,10},{6,9},{7,8},{8,7},{9,6},... | collective-permute-start | bytes 2359304 | tf_op jit(solution)/shard_map/ppermute | solution.py:31
  581.0 2.0 copy-start
  581.0 3.2 copy-start.1
